TPU v7x, 256 devices: a whole 4x4x8 slice. The times are simulated.
256 devices in a mesh: cells: 64 (over z, y, core), cols: 4 (over x).
Axes of the slice: x: 4, y: 4, z: 8, core: 2. Of those that a mesh axis runs over, the one named last changes fastest.
Arguments:
- start_block: float32 [64, 98304], P('cols', 'cells')
- stiffness: float32 [343, 343], replicated
- cell_scale: float32 [4096], P('cells'), may hold values from 0.25 to 2
- node_weight: float32 [343, 4096], P(None, 'cells'), may hold values from -0.25 to 0.75
- cell_count: int32 [64], P('cells'), may hold values from 8 to 64, as said below
- conn: int32 [343, 4096], P(None, 'cells'), may hold values from 0 to 2047, as said below
- send_rows: int32 [128, 256], P('cells'), may hold values from 0 to 1535, as said below
- filter_bounds: float32 [2], replicated, may hold values from 1.2 to 1.6
Outputs:
- filtered: float32 [64, 98304], P('cols', 'cells')
- correlation: float32 [64, 64], P('cells', 'cols')
- projected: float32 [64, 64], P('cells', 'cols')
Inputs may be any that keep to these rules, and one draw needn't show every extreme that they name: `cell_count`: each partition has at least 8 live cells; some partition has exactly 64, some exactly 8. `conn`: entries index the extended rows of the slot's own partition: below 1536 its own nodes, then 256 copies from the left neighbour, then 256 from the right. `send_rows`: for partition p, the list for the left neighbour (row 2p) holds 256 distinct rows of partition p below 768, and the list for the right neighbour (row 2p + 1) holds 256 distinct rows of partition p from 768 on.
All inputs are finite; a program needn't handle non-finite values.
Results may differ from a plain program's by a relative error of at most 0.00025.
Values sent between devices are 32-bit elements; how exact they have to be, the bound alone decides.
A program may use at most 64 MiB of HBM per device.

v0:
```python
import jax
import jax.numpy as jnp
from jax import lax
from jax.sharding import PartitionSpec as P

DEGREE = 4
MULT = 10


def with_halo(cells, sides, width):
    for axis, dim in sides:
        count = lax.axis_size(axis)
        ends = count - 1
        head = lax.slice_in_dim(cells, 0, width, axis=dim)
        tail = lax.slice_in_dim(cells, cells.shape[dim] - width, cells.shape[dim], axis=dim)
        cells = jnp.concatenate(
            [
                lax.ppermute(tail, axis, [(i, (i + 1) % count) for i in range(ends)]),
                cells,
                lax.ppermute(head, axis, [((i + 1) % count, i) for i in range(ends)]),
            ],
            axis=dim,
        )
    return cells


def cell_terms(extended, links, scale, weight, alive, stiffness):
    local = extended[:, links]
    spread = jnp.einsum("ij,bjc->bic", stiffness, local, precision=lax.Precision.HIGHEST)
    terms = (spread * scale[None, None, :] + local * weight[None, :, :]) * (
        alive[None, None, :] / MULT
    )
    return jnp.zeros(extended.shape, jnp.float32).at[:, links].add(terms)


def inner_rows(left, right):
    return lax.dot_general(
        left,
        right,
        (((1,), (1,)), ((), ())),
        precision=lax.Precision.HIGHEST,
        preferred_element_type=jnp.float32,
    )


def per_device(
    start_block, stiffness, cell_scale, node_weight, cell_count, conn, send_rows, filter_bounds
):
    node_dev = start_block.shape[1]
    ghost = send_rows.shape[1]
    slots = jnp.arange(cell_scale.shape[0], dtype=jnp.int32)
    alive = (slots < cell_count[0]).astype(jnp.float32)
    left_rows = send_rows[0]
    right_rows = send_rows[1]
    center = filter_bounds[0]
    half = filter_bounds[1]
    position = lax.axis_index("cells")
    parts_count = lax.axis_size("cells")

    def fill(owned):
        edge = jnp.concatenate([owned[:, left_rows], owned[:, right_rows]], 1)
        padded = with_halo(edge, (("cells", 1),), ghost)
        return jnp.concatenate([owned, padded[:, :ghost], padded[:, -ghost:]], 1)

    def local_terms(extended):
        return cell_terms(extended, conn, cell_scale, node_weight, alive, stiffness)

    def operator(owned):
        pieces = local_terms(fill(owned))
        inner = pieces[:, :node_dev]
        outer = pieces[:, node_dev:]
        back = with_halo(outer, (("cells", 1),), ghost)
        inner = inner.at[:, left_rows].add(back[:, :ghost])
        inner = inner.at[:, right_rows].add(back[:, -ghost:])
        return inner

    previous = start_block
    current = (operator(previous) - center * previous) / half
    for step in range(DEGREE - 1):
        following = 2.0 * ((operator(current) - center * current) / half) - previous
        previous = current
        current = following
    image = operator(current)
    width = current.shape[0]
    total_nodes = parts_count * node_dev
    piece = lax.all_gather(current, "cols", axis=0, tiled=True)
    terms = jnp.concatenate([inner_rows(piece, current), inner_rows(piece, image)], 1) / total_nodes
    summed = lax.psum(terms, "cells")
    rows = summed.shape[0] // parts_count
    result = lax.dynamic_slice_in_dim(summed, position * rows, rows, 0)
    return (current, result[:, :width], result[:, width:])


def solution(mesh):
    placed = (
        P("cols", "cells"),
        P(),
        P("cells"),
        P(None, "cells"),
        P("cells"),
        P(None, "cells"),
        P("cells", None),
        P(),
    )
    return jax.shard_map(
        per_device,
        mesh=mesh,
        in_specs=placed,
        out_specs=(P("cols", "cells"), P("cells", "cols"), P("cells", "cols")),
        check_vma=False,
    )
```

profile of v0, /device:TPU:128, one launch (start us, length us, event | category | flops | bytes accessed | tf_op | source)
XLA Modules:
  0.0 1359.5 jit_solution(3731144741967682279)
XLA Ops:
  15.6 41.0 %gather_fusion.2 = f32[21952,16]{1,0:T(8,128)} fusion(f32[16,2048]{0,1:T(8,128)S(1)} %pad_maximum_fusion, s32[22528]{0:T(1024)S(1)} %pad_clamp_fusion), kind=kCustom, calls=%fused_computation.2 | custom fusion | bytes 2897664 | tf_op jit(solution)/shard_map/gather | solution.py:28
  56.5 9.4 copy.104
  70.3 11.2 copy.132
  81.5 118.0 %scatter_custom_fusion = f32[16,2048]{0,1:T(8,128)S(1)} fusion(s32[21952]{0:T(1024)S(1)} %reshape.264, f32[21952,16]{1,0:T(8,128)} %bitcast.161, f32[]{:T(128)} %constant.10.clone.1), kind=kCustom, calls=%fused_computation.82 | custom fusion | flops 351232 | bytes 131584 | tf_op jit(solution)/shard_map/scatter-add | solution.py:33
  231.4 41.0 %gather_fusion.5 = f32[21952,16]{1,0:T(8,128)} fusion(f32[16,2048]{0,1:T(8,128)S(1)} %pad_maximum_fusion.1, s32[22528]{0:T(1024)S(1)} %pad_clamp_fusion), kind=kCustom, calls=%fused_computation.5 | custom fusion | bytes 2897664 | tf_op jit(solution)/shard_map/gather | solution.py:28
  272.4 10.3 copy.110
  288.8 11.2 copy.135
  300.1 118.0 %scatter_custom_fusion.3 = f32[16,2048]{0,1:T(8,128)S(1)} fusion(s32[21952]{0:T(1024)S(1)} %reshape.264, f32[21952,16]{1,0:T(8,128)} %bitcast.162, f32[]{:T(128)} %constant.10.clone.1), kind=kCustom, calls=%fused_computation.80 | custom fusion | flops 351232 | bytes 131584 | tf_op jit(solution)/shard_map/scatter-add | solution.py:33
  420.1 7.2 collective-permute-start.7
  453.0 41.0 %gather_fusion.8 = f32[21952,16]{1,0:T(8,128)} fusion(f32[16,2048]{0,1:T(8,128)S(1)} %pad_maximum_fusion.2, s32[22528]{0:T(1024)S(1)} %pad_clamp_fusion), kind=kCustom, calls=%fused_computation.8 | custom fusion | bytes 2897664 | tf_op jit(solution)/shard_map/gather | solution.py:28
  493.9 10.3 copy.115
  510.4 11.2 copy.138
  521.6 118.0 %scatter_custom_fusion.6 = f32[16,2048]{0,1:T(8,128)S(1)} fusion(s32[21952]{0:T(1024)S(1)} %reshape.264, f32[21952,16]{1,0:T(8,128)} %bitcast.163, f32[]{:T(128)} %constant.10.clone.1), kind=kCustom, calls=%fused_computation.78 | custom fusion | flops 351232 | bytes 131584 | tf_op jit(solution)/shard_map/scatter-add | solution.py:33
  642.2 7.1 collective-permute-start.11
  675.4 41.0 %gather_fusion.11 = f32[21952,16]{1,0:T(8,128)} fusion(f32[16,2048]{0,1:T(8,128)S(1)} %pad_maximum_fusion.3, s32[22528]{0:T(1024)S(1)} %pad_clamp_fusion), kind=kCustom, calls=%fused_computation.11 | custom fusion | bytes 2897664 | tf_op jit(solution)/shard_map/gather | solution.py:28
  716.3 9.4 copy.119
  730.0 11.2 copy.141
  741.2 118.0 %scatter_custom_fusion.9 = f32[16,2048]{0,1:T(8,128)S(1)} fusion(s32[21952]{0:T(1024)S(1)} %reshape.264, f32[21952,16]{1,0:T(8,128)} %bitcast.164, f32[]{:T(128)} %constant.10.clone.1), kind=kCustom, calls=%fused_computation.76 | custom fusion | flops 351232 | bytes 131584 | tf_op jit(solution)/shard_map/scatter-add | solution.py:33
  891.5 13.2 all_gather.3
  904.8 41.0 %gather_fusion.14 = f32[21952,16]{1,0:T(8,128)} fusion(f32[16,2048]{0,1:T(8,128)S(1)} %pad_maximum_fusion.4, s32[22528]{0:T(1024)S(1)} %pad_clamp_fusion), kind=kCustom, calls=%fused_computation.14 | custom fusion | bytes 2897664 | tf_op jit(solution)/shard_map/gather | solution.py:28
  945.8 10.3 copy.124
  962.2 11.2 copy.144
  973.5 118.0 %scatter_custom_fusion.12 = f32[16,2048]{0,1:T(8,128)S(1)} fusion(s32[21952]{0:T(1024)S(1)} %reshape.264, f32[21952,16]{1,0:T(8,128)} %bitcast.160, f32[]{:T(128)} %constant.10.clone.1), kind=kCustom, calls=%fused_computation.74 | custom fusion | flops 351232 | bytes 131584 | tf_op jit(solution)/shard_map/scatter-add | solution.py:33
  1107.7 250.1 %psum.7 = f32[64,32]{0,1:T(8,128)S(1)} all-reduce(f32[64,32]{0,1:T(8,128)S(1)} %maximum_multiply_fusion), channel_id=1, replica_groups=mesh['cells'=64,'cols'=4] {'cells'}, use_global_device_ids=true, to_apply=%region_15.0 | all-reduce | flops 2048 | bytes 16384 | tf_op jit(solution)/shard_map/psum | solution.py:88
  (125 shorter events, 179.1 us)
Async XLA Ops:
  0.6 65.3 %copy-start = (f32[343,343]{1,0:T(8,128)S(1)}, f32[343,343]{1,0:T(8,128)}, u32[]{:S(2)}) copy-start(f32[343,343]{1,0:T(8,128)} %param.9) | copy-start | bytes 1411792
  3.3 12.0 collective-permute-start
  6.0 9.5 collective-permute-start.1
  81.5 127.7 %copy-start.8 = (f32[16,1536]{1,0:T(8,128)S(1)}, f32[16,1536]{1,0:T(8,128)}, u32[]{:S(2)}) copy-start(f32[16,1536]{1,0:T(8,128)} %param.8) | copy-start | bytes 294916
  200.2 10.0 collective-permute-start.2
  202.1 10.7 collective-permute-start.3
  220.0 9.6 collective-permute-start.4
  221.9 9.5 collective-permute-start.5
  418.1 11.3 collective-permute-start.6
  420.0 17.4 %copy-start.2 = (f32[16,1536]{0,1:T(8,128)S(1)}, f32[16,1536]{0,1:T(8,128)}, u32[]{:S(2)}) copy-start(f32[16,1536]{0,1:T(8,128)} %copy-done.1) | copy-start | bytes 294916
  420.1 13.6 collective-permute-start.7
  441.5 9.6 collective-permute-start.8
  443.4 9.5 collective-permute-start.9
  640.3 10.0 collective-permute-start.10
  642.2 12.2 collective-permute-start.11
  662.8 9.6 collective-permute-start.12
  664.7 9.5 collective-permute-start.13
  860.0 10.0 collective-permute-start.14
  861.9 12.3 collective-permute-start.15
  881.1 64.6 %copy-start.9 = (f32[16,1536]{1,0:T(8,128)}, f32[16,1536]{1,0:T(8,128)S(1)}, u32[]{:S(2)}) copy-start(f32[16,1536]{1,0:T(8,128)S(1)} %copy.127) | copy-start | bytes 294916
  882.6 22.1 %collective-permute-start.16 = (f32[16,256]{0,1:T(8,128)S(1)}, f32[16,256]{0,1:T(8,128)S(1)}, u32[]{:S(2)}, u32[]{:S(2)}) collective-permute-start(f32[16,256]{0,1:T(8,128)S(1)} %bitcast.183), channel_id=1, source_target_pairs={{0,4},{4,8},{8,12},{12,16},{16,20},{20,24},{24,28},{28,32},{32,36}... | collective-permute-start | bytes 49160 | tf_op jit(solution)/shard_map/ppermute | solution.py:18
  884.5 20.2 %collective-permute-start.17 = (f32[16,256]{0,1:T(8,128)S(1)}, f32[16,256]{0,1:T(8,128)S(1)}, u32[]{:S(2)}, u32[]{:S(2)}) collective-permute-start(f32[16,256]{0,1:T(8,128)S(1)} %bitcast.179), channel_id=1, source_target_pairs={{4,0},{8,4},{12,8},{16,12},{20,16},{24,20},{28,24},{32,28},{36,32}... | collective-permute-start | bytes 49160 | tf_op jit(solution)/shard_map/ppermute | solution.py:20
  1091.5 10.3 collective-permute-start.18
  1093.4 10.7 collective-permute-start.19
  (8 other events, 69.2 us)
where the time goes:
time: 1370 us; the launch traced here: 1360 us
  other arithmetic  638 us (47%)
  local copies, waits for them, and re-layouts  329 us (24%)
  blocking collectives  263 us (19%)
  starting transfers between devices  89.4 us (7%)
  matrix products  29.9 us (2%)
    scatter-add x5, other arithmetic, cell_terms(): return jnp.zeros(extended.shape, jnp.float32).at[:, links].add(terms)  590 us
    gather x10, local copies, waits for them, and re-layouts, cell_terms(): local = extended[:, links]  254 us
    psum x1, blocking collectives, per_device(): summed = lax.psum(terms, 'cells')  250 us
    ppermute x10, starting transfers between devices, with_halo(): lax.ppermute(head, axis, [((i + 1) % count, i) for i in range(ends)])  70.3 us
    mul x5, local copies, waits for them, and re-layouts, cell_terms(): (spread * scale[None, None, :] + local * weight[None, :, :]) * (alive[Non...  56.2 us
  transfers between devices with their start and end apart: 20, of which 8 were waited for; matrix products, arithmetic and copies ran while one was open for 2% of the time, Pallas kernels for 0%

commit v1 on v0

v1 whole, which is shorter than its diff:
```python
import functools

import jax
import jax.numpy as jnp
from jax import lax
from jax.experimental import pallas as pl
from jax.experimental.pallas import tpu as pltpu
from jax.sharding import PartitionSpec as P

DEGREE = 4
MULT = 10
LANES = 128
CHUNK = 8
BF16 = jnp.bfloat16
F32 = jnp.float32
I32 = jnp.int32
MESH = pl.DeviceIdType.MESH


def iota(shape, dim):
    return lax.broadcasted_iota(I32, shape, dim)


def split(x):
    high = x.astype(BF16)
    return high, (x - high.astype(F32)).astype(BF16)


def dot(a, b):
    return jnp.dot(a, b, preferred_element_type=F32)


def dot_nt(a, b):
    return lax.dot_general(a, b, (((1,), (1,)), ((), ())), preferred_element_type=F32)


def pick(x, index):
    return jnp.take_along_axis(x, index, axis=1, mode="promise_in_bounds")


def mark(condition):
    return jnp.where(condition, 1.0, 0.0).astype(F32)


def kernel(
    cfg,
    start,
    stiff,
    scale,
    weight,
    count,
    conn,
    send,
    bounds,
    out_filtered,
    out_corr,
    out_proj,
    kpad,
    kk,
    ci,
    newc,
    newr,
    tab,
    rows_nm,
    wt,
    sc,
    onehot,
    masks,
    vcur,
    vprev,
    image,
    xa,
    xb,
    amat,
    acc,
    part,
    from_left,
    from_right,
    gath,
    gsum,
    got1,
    mid,
    got2,
    ssem,
    rsem,
    gssem,
    grsem,
    s1sem,
    r1sem,
    s2sem,
    r2sem,
):
    width, owned, ghost, npc, cells, parts, cols, inner = cfg
    slots = kk.shape[0]
    groups = (owned + 2 * ghost) // ghost
    half = groups * width
    tiles = 2 * groups
    near = inner
    far = parts // inner

    p = lax.axis_index("cells")
    q = lax.axis_index("cols")
    left = lax.rem(p + parts - 1, parts)
    right = lax.rem(p + 1, parts)
    z = lax.div(p, near)
    yc = lax.rem(p, near)

    far_peers = [lax.rem(z + d, far) * near + yc for d in range(1, far)]
    near_peers = [z * near + lax.rem(yc + d, near) for d in range(1, near)]
    col_peers = [lax.rem(q + d, cols) for d in range(1, cols)]

    barrier = pltpu.get_barrier_semaphore()
    targets = [(left, q), (right, q)]
    targets += [(p, other) for other in col_peers]
    targets += [(other, q) for other in far_peers]
    targets += [(other, q) for other in near_peers]
    for target in targets:
        pl.semaphore_signal(barrier, inc=1, device_id=target, device_id_type=MESH)

    kpad[...] = jnp.zeros_like(kpad)
    kpad[0:npc, 0:npc] = stiff[...]
    k_high, k_low = split(kpad[...].T)
    kk[:, 0:slots] = k_high
    kk[:, slots:] = k_low

    lane = iota((1, LANES), 1)
    per_side = owned // 2 // LANES
    rows_nm[...] = jnp.zeros_like(rows_nm)
    places = []
    for side in range(2):
        column = jnp.broadcast_to(send[side : side + 1, :].astype(F32), (LANES, ghost)).T
        order = (iota((ghost, LANES), 0) + 1).astype(F32)
        for t in range(per_side):
            tile = side * per_side + t
            here = (iota((ghost, LANES), 1) + tile * LANES).astype(F32)
            place = jnp.sum(jnp.where(column == here, order, 0.0), axis=0, keepdims=True)
            places.append(place)
            rows_nm[tile : tile + 1, :] = mark(place == 0.0)
    free = rows_nm[...].astype(BF16)
    before = mark(iota((LANES, LANES), 0) < iota((LANES, LANES), 1)).astype(BF16)
    above = mark(iota((LANES, LANES), 0) > iota((LANES, LANES), 1)).astype(BF16)
    ones = jnp.ones((LANES, LANES), BF16)
    rank = dot(free, before) + dot(above, dot(free, ones).astype(BF16))
    base = (ghost, owned)
    for tile in range(2 * per_side):
        place = places[tile]
        shared = place + float(base[tile // per_side] - 1)
        inside = rank[tile : tile + 1, :] + float(2 * ghost)
        tab[tile : tile + 1, :] = jnp.where(place > 0.0, shared, inside).astype(I32)
    for t in range(ghost // LANES):
        a = 2 * per_side + t
        b = a + ghost // LANES
        tab[a : a + 1, :] = lane + t * LANES
        tab[b : b + 1, :] = lane + (owned + ghost + t * LANES)

    ci[...] = jnp.zeros_like(ci)
    ci[0:npc, 0:cells] = conn[...]
    block = 64

    @pl.loop(0, slots // block)
    def _(i):
        rows = pl.ds(pl.multiple_of(i * block, block), block)
        index = ci[rows, :]
        low = index & (LANES - 1)
        tile = index >> 7
        value = None
        for t in range(tiles):
            got = pick(jnp.broadcast_to(tab[t : t + 1, :], (block, LANES)), low)
            value = got if value is None else jnp.where(tile == t, got, value)
        newc[rows, :] = value

    newr[...] = newc[...].astype(F32).T.astype(I32)

    live = mark(iota((LANES, slots), 0) < count[0, 0]) * (1.0 / MULT)
    kpad[:, 0:LANES] = jnp.zeros((slots, LANES), F32)
    kpad[0:npc, 0:cells] = weight[...]
    wt[...] = kpad[:, 0:LANES].T * live
    scale_row = jnp.concatenate([scale[...], jnp.zeros((1, LANES - cells), F32)], axis=1)
    scale_col = jnp.broadcast_to(scale_row, (LANES, LANES)).T
    sc[...] = jnp.concatenate([scale_col] * (slots // LANES), axis=1) * live

    @pl.loop(0, cells)
    def _(c):
        column = pick(newc[...] & (ghost - 1), jnp.full((slots, LANES), c, I32))
        rows = pl.ds(pl.multiple_of(c * slots, slots), slots)
        for t in range(ghost // LANES):
            hit = mark(column == iota((slots, LANES), 1) + t * LANES)
            onehot[rows, t * LANES : (t + 1) * LANES] = hit.astype(BF16)
        group = jnp.broadcast_to(newr[pl.ds(c, 1), :] >> 8, (half, slots))
        member = mark(group == iota((half, slots), 0) // width)
        masks[pl.ds(pl.multiple_of(c * half, half), half), :] = member.astype(BF16)

    tab_cols = jnp.concatenate([tab[...], jnp.zeros((LANES - tiles, LANES), I32)], axis=0).astype(F32).T.astype(I32)
    total = jnp.zeros((2 * half, ghost), F32)
    for t in range(owned // LANES):
        high, low = split(start[:, t * LANES : (t + 1) * LANES])
        group = jnp.broadcast_to(tab[t : t + 1, :] >> 8, (half, LANES))
        member = mark(group == iota((half, LANES), 0) // width).astype(BF16)
        left_side = jnp.concatenate(
            [jnp.concatenate([high] * groups, axis=0) * member, jnp.concatenate([low] * groups, axis=0) * member], axis=0
        )
        column = jnp.broadcast_to(tab_cols[:, t : t + 1] & (ghost - 1), (LANES, ghost))
        total += dot(left_side, mark(column == iota((LANES, ghost), 1)).astype(BF16))
    part[0] = total[0:half] + total[half:]

    pl.semaphore_wait(barrier, len(targets))

    has_left = jnp.where(p > 0, 1.0, 0.0).astype(F32)
    has_right = jnp.where(p < parts - 1, 1.0, 0.0).astype(F32)
    pair = 2 * width

    def exchange(step):
        to_left = pltpu.make_async_remote_copy(
            src_ref=part.at[step, pl.ds(0, pair)],
            dst_ref=from_right.at[step],
            send_sem=ssem.at[0, step],
            recv_sem=rsem.at[0, step],
            device_id=(left, q),
            device_id_type=MESH,
        )
        to_right = pltpu.make_async_remote_copy(
            src_ref=part.at[step, pl.ds(half - pair, pair)],
            dst_ref=from_left.at[step],
            send_sem=ssem.at[1, step],
            recv_sem=rsem.at[1, step],
            device_id=(right, q),
            device_id_type=MESH,
        )
        to_left.start()
        to_right.start()
        to_left.wait()
        to_right.wait()
        a = part[step, 0:width, :] + from_left[step, 0:width, :]
        b = part[step, width:pair, :] + from_left[step, width:pair, :] * has_left
        c = part[step, half - pair : half - width, :] + from_right[step, 0:width, :] * has_right
        d = part[step, half - width : half, :] + from_right[step, width:pair, :]
        return jnp.concatenate([a * has_left, b, part[step, pair : half - pair, :], c, d * has_right], axis=0)

    def gather(chunk, dest):
        for c in range(CHUNK):
            row = newr[pl.ds(chunk * CHUNK + c, 1), :]
            for l in range(slots // LANES):
                index = jnp.broadcast_to(row[:, l * LANES : (l + 1) * LANES], (width, LANES))
                low = index & (LANES - 1)
                tile = index >> 7
                value = None
                for t in range(tiles):
                    source = vcur[(t // 2) * width : (t // 2 + 1) * width, (t % 2) * LANES : (t % 2 + 1) * LANES]
                    got = pick(source, low)
                    value = got if value is None else jnp.where(tile == t, got, value)
                dest[c * width : (c + 1) * width, l * LANES : (l + 1) * LANES] = value

    def process(chunk, x):
        high, low = split(x[...])
        wide = dot(high, kk[...])
        spread = wide[:, 0:slots] + wide[:, slots:] + dot(low, kk[:, 0:slots])
        for c in range(CHUNK):
            cell = chunk * CHUNK + c
            rows = slice(c * width, (c + 1) * width)
            term = spread[rows] * sc[pl.ds(cell, 1), :] + x[rows, :] * wt[pl.ds(cell, 1), :]
            high, low = split(term)
            for g in range(groups):
                member = masks[pl.ds(pl.multiple_of(cell * half + g * width, width), width), :]
                amat[g * width : (g + 1) * width, c * slots : (c + 1) * slots] = high * member
                amat[half + g * width : half + (g + 1) * width, c * slots : (c + 1) * slots] = low * member
        span = CHUNK * slots
        acc[...] += dot(amat[...], onehot[pl.ds(pl.multiple_of(chunk * span, span), span), :])

    def gather_copy(d):
        return pltpu.make_async_remote_copy(
            src_ref=gath.at[0],
            dst_ref=gath.at[d],
            send_sem=gssem.at[d],
            recv_sem=grsem.at[d],
            device_id=(p, col_peers[d - 1]),
            device_id_type=MESH,
        )

    vcur[...] = exchange(0)
    vprev[...] = jnp.zeros_like(vprev)
    center = bounds[0, 0]
    inverse = 1.0 / jnp.full((1, ghost), bounds[0, 1], F32)
    chunks = cells // CHUNK

    @pl.loop(1, DEGREE + 2)
    def _(step):
        acc[...] = jnp.zeros_like(acc)
        gather(0, xa)

        @pl.loop(0, chunks // 2)
        def _(i):
            gather(2 * i + 1, xb)
            process(2 * i, xa)
            gather(lax.rem(2 * i + 2, chunks), xa)
            process(2 * i + 1, xb)

        part[step] = acc[0:half, :] + acc[half:, :]
        applied = exchange(step)
        image[...] = applied

        @pl.when(step <= DEGREE)
        def _():
            current = vcur[...]
            factor = inverse * jnp.where(step > 1, 2.0, 1.0).astype(F32)
            following = (applied - center * current) * factor - vprev[...]
            vprev[...] = current
            vcur[...] = following

        @pl.when(step == DEGREE)
        def _():
            gath[0] = vcur[width : half - width, :]
            for d in range(1, cols):
                gather_copy(d).start()

    for t in range(owned // LANES):
        index = jnp.broadcast_to(tab[t : t + 1, :], (width, LANES))
        low = index & (LANES - 1)
        tile = index >> 7
        value = None
        for s in range(2, tiles - 2):
            source = vcur[(s // 2) * width : (s // 2 + 1) * width, (s % 2) * LANES : (s % 2 + 1) * LANES]
            got = pick(source, low)
            value = got if value is None else jnp.where(tile == s, got, value)
        out_filtered[:, t * LANES : (t + 1) * LANES] = value

    for d in range(1, cols):
        gather_copy(d).wait()

    gram = [jnp.zeros((width, 2 * width), F32) for _ in range(cols)]
    for g in range(groups - 2):
        rows = slice(g * width, (g + 1) * width)
        mine = jnp.concatenate([gath[0, rows, :], image[(g + 1) * width : (g + 2) * width, :]], axis=0)
        all_rows = jnp.concatenate([gath[d, rows, :] for d in range(cols)], axis=0)
        mine_high, mine_low = split(mine)
        all_high, all_low = split(all_rows)
        term = dot_nt(all_high, mine_high) + dot_nt(all_high, mine_low) + dot_nt(all_low, mine_high)
        gram = [gram[d] + term[d * width : (d + 1) * width] for d in range(cols)]
    gsum[...] = jnp.zeros_like(gsum)
    for d in range(cols):
        group = lax.rem(q + cols - d, cols)
        gsum[pl.ds(pl.multiple_of(group * width, width), width), 0 : 2 * width] = gram[d] * (1.0 / (parts * owned))

    def far_copy(d):
        block = lax.rem(z + d, far) * near
        return pltpu.make_async_remote_copy(
            src_ref=gsum.at[pl.ds(pl.multiple_of(block, near), near)],
            dst_ref=got1.at[d],
            send_sem=s1sem.at[d],
            recv_sem=r1sem.at[d],
            device_id=(far_peers[d - 1], q),
            device_id_type=MESH,
        )

    def near_copy(d):
        return pltpu.make_async_remote_copy(
            src_ref=mid,
            dst_ref=got2.at[d],
            send_sem=s2sem.at[d],
            recv_sem=r2sem.at[d],
            device_id=(near_peers[d - 1], q),
            device_id_type=MESH,
        )

    for d in range(1, far):
        far_copy(d).start()
    value = gsum[pl.ds(pl.multiple_of(z * near, near), near), :]
    for d in range(1, far):
        far_copy(d).wait()
        value += got1[d]
    mid[...] = value
    for d in range(1, near):
        near_copy(d).start()
    for d in range(1, near):
        near_copy(d).wait()
        value += got2[d]
    got2[0] = value
    row = got2[0, pl.ds(yc, 1), :]
    out_corr[...] = row[:, 0:width]
    out_proj[...] = row[:, width : 2 * width]


def per_device(
    start_block, stiffness, cell_scale, node_weight, cell_count, conn, send_rows, filter_bounds
):
    width, owned = start_block.shape
    ghost = send_rows.shape[1]
    npc, cells = conn.shape
    parts = lax.axis_size("cells")
    cols = lax.axis_size("cols")
    inner = parts // 8
    slots = -(-npc // LANES) * LANES
    half = (owned + 2 * ghost) // ghost * width
    steps = DEGREE + 2
    cfg = (width, owned, ghost, npc, cells, parts, cols, inner)
    far = parts // inner
    vmem = pl.BlockSpec(memory_space=pltpu.VMEM)
    smem = pl.BlockSpec(memory_space=pltpu.SMEM)
    dma = pltpu.SemaphoreType.DMA
    rows = parts * width // parts * cols // parts
    return pl.pallas_call(
        functools.partial(kernel, cfg),
        out_shape=(
            jax.ShapeDtypeStruct((width, owned), F32),
            jax.ShapeDtypeStruct((rows, width), F32),
            jax.ShapeDtypeStruct((rows, width), F32),
        ),
        in_specs=[vmem, vmem, vmem, vmem, smem, vmem, vmem, smem],
        out_specs=(vmem, vmem, vmem),
        scratch_shapes=[
            pltpu.VMEM((slots, slots), F32),
            pltpu.VMEM((slots, 2 * slots), BF16),
            pltpu.VMEM((slots, LANES), I32),
            pltpu.VMEM((slots, LANES), I32),
            pltpu.VMEM((LANES, slots), I32),
            pltpu.VMEM((16, LANES), I32),
            pltpu.VMEM((LANES, LANES), F32),
            pltpu.VMEM((LANES, slots), F32),
            pltpu.VMEM((LANES, slots), F32),
            pltpu.VMEM((cells * slots, ghost), BF16),
            pltpu.VMEM((cells * half, slots), BF16),
            pltpu.VMEM((half, ghost), F32),
            pltpu.VMEM((half, ghost), F32),
            pltpu.VMEM((half, ghost), F32),
            pltpu.VMEM((CHUNK * width, slots), F32),
            pltpu.VMEM((CHUNK * width, slots), F32),
            pltpu.VMEM((2 * half, CHUNK * slots), BF16),
            pltpu.VMEM((2 * half, ghost), F32),
            pltpu.VMEM((steps, half, ghost), F32),
            pltpu.VMEM((steps, 2 * width, ghost), F32),
            pltpu.VMEM((steps, 2 * width, ghost), F32),
            pltpu.VMEM((cols, half - 2 * width, ghost), F32),
            pltpu.VMEM((width * cols, LANES), F32),
            pltpu.VMEM((far, inner, LANES), F32),
            pltpu.VMEM((inner, LANES), F32),
            pltpu.VMEM((inner, inner, LANES), F32),
            dma((2, steps)),
            dma((2, steps)),
            dma((cols,)),
            dma((cols,)),
            dma((far,)),
            dma((far,)),
            dma((inner,)),
            dma((inner,)),
        ],
        compiler_params=pltpu.CompilerParams(
            collective_id=0, has_side_effects=True, vmem_limit_bytes=52 * 1024 * 1024
        ),
    )(
        start_block,
        stiffness,
        cell_scale.reshape(1, cells),
        node_weight,
        cell_count.reshape(1, 1),
        conn,
        send_rows,
        filter_bounds.reshape(1, 2),
    )


def solution(mesh):
    placed = (
        P("cols", "cells"),
        P(),
        P("cells"),
        P(None, "cells"),
        P("cells"),
        P(None, "cells"),
        P("cells", None),
        P(),
    )
    return jax.shard_map(
        per_device,
        mesh=mesh,
        in_specs=placed,
        out_specs=(P("cols", "cells"), P("cells", "cols"), P("cells", "cols")),
        check_vma=False,
    )
```

time: 1370 us -> 113 us (0.08)
  the two profiles are of different devices: /device:TPU:128 before, /device:TPU:1 now
where the time goes in v1:
time: 113 us
  Pallas kernels  107 us (95%)
  local copies, waits for them, and re-layouts  4.61 us (4%)
  between operations  1.42 us (1%)
    pallas_call x1, Pallas kernels, per_device(): pl.pallas_call(functools.partial(kernel, cfg), out_shape=(jax.ShapeDtypeS...  107 us
    unnamed x15, local copies, waits for them, and re-layouts  4.61 us

profile of v1, /device:TPU:1, one launch (start us, length us, event | category | flops | bytes accessed | tf_op | source)
XLA Modules:
  0.0 113.2 jit_solution(6191851060563273083)
XLA Ops:
  0.6 0.0 copy-start
  1.3 1.0 copy.11.weight
  2.4 0.0 copy-start.2
  2.4 0.0 copy-start.3
  2.4 0.0 copy-start.4
  2.4 1.0 copy.12.conn
  3.4 0.0 copy-done
  3.4 0.0 copy-done.2
  3.4 0.0 copy-done.3
  3.4 0.0 copy-done.4
  3.5 0.0 copy-start.1
  3.5 0.9 copy-done.1
  4.4 107.2 %shard_map.103 = (f32[16,1536]{1,0:T(8,128)S(1)}, f32[1,16]{1,0:T(1,128)S(1)}, f32[1,16]{1,0:T(1,128)S(1)}) custom-call(f32[16,1536]{1,0:T(8,128)S(1)} %copy-done.1, f32[343,343]{1,0:T(8,128)S(1)} %copy-done, f32[1,64]{1,0:T(1,128)S(1)} %bitcast.4, f32[343,64]{1,0:T(8,128)S(1)} %copy.11.weight, s32[1,1]{1,0:T(1,128)} %bitcast.3.count, ...), custom_call_target="tpu_custom_call" | custom-call | tf_op jit(solution)/shard_map/pallas_call | solution.py:400
  111.6 0.6 copy.17
  112.2 0.5 copy.18
  112.7 0.5 copy.19
Async XLA Ops:
  0.6 2.8 %copy-start = (f32[343,343]{1,0:T(8,128)S(1)}, f32[343,343]{1,0:T(8,128)}, u32[]{:S(2)}) copy-start(f32[343,343]{1,0:T(8,128)} %stiff.1) | copy-start | bytes 1411792
  2.4 1.1 copy-start.2
  2.4 1.1 copy-start.3
  2.4 1.1 copy-start.4
  3.5 0.9 copy-start.1

commit v2 on v1

v2 whole, which is shorter than its diff:
```python
import functools

import jax
import jax.numpy as jnp
from jax import lax
from jax.experimental import pallas as pl
from jax.experimental.pallas import tpu as pltpu
from jax.sharding import PartitionSpec as P

DEGREE = 4
MULT = 10
LANES = 128
CHUNK = 8
BF16 = jnp.bfloat16
F32 = jnp.float32
I32 = jnp.int32
MESH = pl.DeviceIdType.MESH


def iota(shape, dim):
    return lax.broadcasted_iota(I32, shape, dim)


def split(x):
    high = x.astype(BF16)
    return high, (x - high.astype(F32)).astype(BF16)


def dot(a, b):
    return jnp.dot(a, b, preferred_element_type=F32)


def dot_nt(a, b):
    return lax.dot_general(a, b, (((1,), (1,)), ((), ())), preferred_element_type=F32)


def pick(x, index):
    return jnp.take_along_axis(x, index, axis=1, mode="promise_in_bounds")


def mark(condition):
    return jnp.where(condition, 1.0, 0.0).astype(F32)


def kernel(
    cfg,
    start,
    stiff,
    scale,
    weight,
    count,
    conn,
    send,
    bounds,
    out_filtered,
    out_corr,
    out_proj,
    kpad,
    kk,
    newr,
    tab,
    rows_nm,
    wt,
    sc,
    onehot,
    masks,
    vcur,
    vprev,
    xall,
    xa,
    xb,
    aa,
    ab,
    acc,
    part,
    from_left,
    from_right,
    gath,
    gsum,
    got1,
    mid,
    got2,
    ssem,
    rsem,
    gssem,
    grsem,
    s1sem,
    r1sem,
    s2sem,
    r2sem,
):
    width, owned, ghost, npc, cells, parts, cols, inner = cfg
    slots = newr.shape[1]
    groups = (owned + 2 * ghost) // ghost
    half = groups * width
    tiles = 2 * groups
    near = inner
    far = parts // inner
    pair = 2 * width
    chunks = cells // CHUNK
    span = CHUNK * slots

    p = lax.axis_index("cells")
    q = lax.axis_index("cols")
    left = lax.rem(p + parts - 1, parts)
    right = lax.rem(p + 1, parts)
    z = lax.div(p, near)
    yc = lax.rem(p, near)

    far_peers = [lax.rem(z + d, far) * near + yc for d in range(1, far)]
    near_peers = [z * near + lax.rem(yc + d, near) for d in range(1, near)]
    col_peers = [lax.rem(q + d, cols) for d in range(1, cols)]

    barrier = pltpu.get_barrier_semaphore()
    targets = [(left, q), (right, q)]
    targets += [(p, other) for other in col_peers]
    targets += [(other, q) for other in far_peers]
    targets += [(other, q) for other in near_peers]
    for target in targets:
        pl.semaphore_signal(barrier, inc=1, device_id=target, device_id_type=MESH)

    lane = iota((1, LANES), 1)
    per_side = owned // 2 // LANES
    rows_nm[...] = jnp.zeros_like(rows_nm)
    places = []
    for side in range(2):
        column = jnp.broadcast_to(send[side : side + 1, :].astype(F32), (LANES, ghost)).T
        order = (iota((ghost, LANES), 0) + 1).astype(F32)
        for t in range(per_side):
            tile = side * per_side + t
            here = (iota((ghost, LANES), 1) + tile * LANES).astype(F32)
            place = jnp.sum(jnp.where(column == here, order, 0.0), axis=0, keepdims=True)
            places.append(place)
            rows_nm[tile : tile + 1, :] = mark(place == 0.0)
    free = rows_nm[...].astype(BF16)
    before = mark(iota((LANES, LANES), 0) < iota((LANES, LANES), 1)).astype(BF16)
    above = mark(iota((LANES, LANES), 0) > iota((LANES, LANES), 1)).astype(BF16)
    ones = jnp.ones((LANES, LANES), BF16)
    rank = dot(free, before) + dot(above, dot(free, ones).astype(BF16))
    base = (ghost, owned)
    for tile in range(2 * per_side):
        place = places[tile]
        shared = place + float(base[tile // per_side] - 1)
        inside = rank[tile : tile + 1, :] + float(2 * ghost)
        tab[tile : tile + 1, :] = jnp.where(place > 0.0, shared, inside).astype(I32)
    for t in range(ghost // LANES):
        a = 2 * per_side + t
        b = a + ghost // LANES
        tab[a : a + 1, :] = lane + t * LANES
        tab[b : b + 1, :] = lane + (owned + ghost + t * LANES)

    tab_cols = jnp.concatenate([tab[...], jnp.zeros((LANES - tiles, LANES), I32)], axis=0).astype(F32).T.astype(I32)
    total = jnp.zeros((2 * half, ghost), F32)
    for t in range(owned // LANES):
        high, low = split(start[:, t * LANES : (t + 1) * LANES])
        group = jnp.broadcast_to(tab[t : t + 1, :] >> 8, (half, LANES))
        member = mark(group == iota((half, LANES), 0) // width).astype(BF16)
        left_side = jnp.concatenate(
            [jnp.concatenate([high] * groups, axis=0) * member, jnp.concatenate([low] * groups, axis=0) * member], axis=0
        )
        column = jnp.broadcast_to(tab_cols[:, t : t + 1] & (ghost - 1), (LANES, ghost))
        total += dot(left_side, mark(column == iota((LANES, ghost), 1)).astype(BF16))
    part[0] = total[0:half] + total[half:]

    def to_left(step):
        return pltpu.make_async_remote_copy(
            src_ref=part.at[step, pl.ds(0, pair)],
            dst_ref=from_right.at[step],
            send_sem=ssem.at[0, step],
            recv_sem=rsem.at[0, step],
            device_id=(left, q),
            device_id_type=MESH,
        )

    def to_right(step):
        return pltpu.make_async_remote_copy(
            src_ref=part.at[step, pl.ds(half - pair, pair)],
            dst_ref=from_left.at[step],
            send_sem=ssem.at[1, step],
            recv_sem=rsem.at[1, step],
            device_id=(right, q),
            device_id_type=MESH,
        )

    def begin(step):
        to_left(step).start()
        to_right(step).start()

    has_left = jnp.where(p > 0, 1.0, 0.0).astype(F32)
    has_right = jnp.where(p < parts - 1, 1.0, 0.0).astype(F32)
    center = bounds[0, 0]
    inverse = 1.0 / jnp.full((1, ghost), bounds[0, 1], F32)

    def advance(step, rows, applied):
        current = vcur[rows, :]
        doubled = jnp.where(step > 1, 2.0, 1.0).astype(F32)
        first = jnp.where(step > 0, 0.0, 1.0).astype(F32)
        factor = inverse * (doubled * (1.0 - first)) + first
        following = (applied - (center * (1.0 - first)) * current) * factor - vprev[rows, :]
        vprev[rows, :] = current
        vcur[rows, :] = following

    def finish(step):
        to_left(step).wait()
        to_right(step).wait()
        a = (part[step, 0:width, :] + from_left[step, 0:width, :]) * has_left
        b = part[step, width:pair, :] + from_left[step, width:pair, :] * has_left
        advance(step, slice(0, pair), jnp.concatenate([a, b], axis=0))
        c = part[step, half - pair : half - width, :] + from_right[step, 0:width, :] * has_right
        d = (part[step, half - width : half, :] + from_right[step, width:pair, :]) * has_right
        advance(step, slice(half - pair, half), jnp.concatenate([c, d], axis=0))

    pl.semaphore_wait(barrier, len(targets))
    begin(0)
    vcur[...] = jnp.zeros_like(vcur)
    vprev[...] = jnp.zeros_like(vprev)
    advance(0, slice(pair, half - pair), part[0, pair : half - pair, :])

    kpad[...] = jnp.zeros_like(kpad)
    kpad[0:npc, 0:npc] = stiff[...]
    k_high, k_low = split(kpad[...].T)
    kk[0:slots, :] = k_high
    kk[slots : 2 * slots, :] = k_high
    kk[2 * slots :, :] = k_low

    newr[...] = jnp.zeros_like(newr)
    newr[:, 0:npc] = conn[...]
    for l in range(slots // LANES):
        index = newr[:, l * LANES : (l + 1) * LANES]
        low = index & (LANES - 1)
        tile = index >> 7
        value = None
        for t in range(tiles):
            got = pick(jnp.broadcast_to(tab[t : t + 1, :], (cells, LANES)), low)
            value = got if value is None else jnp.where(tile == t, got, value)
        newr[:, l * LANES : (l + 1) * LANES] = value

    live = mark(iota((cells, slots), 0) < count[0, 0]) * (1.0 / MULT)
    wt[...] = jnp.zeros_like(wt)
    wt[:, 0:npc] = weight[...]
    wt[...] = wt[...] * live
    scale_row = jnp.concatenate([scale[...], jnp.zeros((1, LANES - cells), F32)], axis=1)
    scale_col = jnp.broadcast_to(scale_row, (LANES, LANES)).T
    sc[...] = jnp.concatenate([scale_col[0:cells]] * (slots // LANES), axis=1) * live

    @pl.loop(0, cells)
    def _(c):
        index = newr[pl.ds(c, 1), :]
        place = (index & (ghost - 1)).astype(F32).astype(BF16)
        hit = jnp.broadcast_to(place, (ghost, slots)) == iota((ghost, slots), 0).astype(F32).astype(BF16)
        onehot[:, pl.ds(pl.multiple_of(c * slots, LANES), slots)] = jnp.where(
            hit, jnp.ones((), BF16), jnp.zeros((), BF16)
        )
        group = (index >> 8).astype(F32).astype(BF16)
        member = jnp.broadcast_to(group, (half, slots)) == (iota((half, slots), 0) // width).astype(F32).astype(BF16)
        masks[pl.ds(pl.multiple_of(c * half, half), half), :] = jnp.where(
            member, jnp.ones((), BF16), jnp.zeros((), BF16)
        )

    inner_tiles = range(4, tiles - 4)
    outer_tiles = list(range(4)) + list(range(tiles - 4, tiles))

    def collect(cell, group, which, value):
        index = jnp.broadcast_to(newr[pl.ds(cell, 1), :][:, group * LANES : (group + 1) * LANES], (width, LANES))
        low = index & (LANES - 1)
        tile = index >> 7
        for t in which:
            source = vcur[(t // 2) * width : (t // 2 + 1) * width, (t % 2) * LANES : (t % 2 + 1) * LANES]
            value = jnp.where(tile == t, pick(source, low), value)
        return value

    def rows_of(cell):
        return pl.ds(pl.multiple_of(cell * width, width), width)

    def gather_inner(chunk):
        for c in range(CHUNK):
            cell = chunk * CHUNK + c
            for l in range(slots // LANES):
                value = collect(cell, l, inner_tiles, jnp.zeros((width, LANES), F32))
                xall[rows_of(cell), l * LANES : (l + 1) * LANES] = value

    def gather_outer(chunk, x):
        for c in range(CHUNK):
            cell = chunk * CHUNK + c
            for l in range(slots // LANES):
                cut = slice(l * LANES, (l + 1) * LANES)
                x[c * width : (c + 1) * width, cut] = collect(cell, l, outer_tiles, xall[rows_of(cell), cut])

    def spread(chunk, x, a):
        local = x[...]
        high, low = split(local)
        wide = dot(jnp.concatenate([high, low, high], axis=1), kk[...])
        for c in range(CHUNK):
            cell = chunk * CHUNK + c
            rows = slice(c * width, (c + 1) * width)
            term = wide[rows] * sc[pl.ds(cell, 1), :] + local[rows] * wt[pl.ds(cell, 1), :]
            high, low = split(term)
            for g in range(groups):
                member = masks[pl.ds(pl.multiple_of(cell * half + g * width, width), width), :]
                a[g * width : (g + 1) * width, c * slots : (c + 1) * slots] = high * member
                a[half + g * width : half + (g + 1) * width, c * slots : (c + 1) * slots] = low * member

    def scatter(chunk, a):
        acc[...] += dot_nt(a[...], onehot[:, pl.ds(pl.multiple_of(chunk * span, LANES), span)])

    def gather_copy(d):
        return pltpu.make_async_remote_copy(
            src_ref=vcur,
            dst_ref=gath.at[d - 1],
            send_sem=gssem.at[d],
            recv_sem=grsem.at[d],
            device_id=(p, col_peers[d - 1]),
            device_id_type=MESH,
        )

    last = DEGREE + 1

    @pl.loop(1, last + 1)
    def _(step):
        @pl.loop(0, chunks)
        def _(i):
            gather_inner(i)

        finish(step - 1)

        @pl.when(step == last)
        def _():
            for d in range(1, cols):
                gather_copy(d).start()

        acc[...] = jnp.zeros_like(acc)
        gather_outer(0, xa)
        gather_outer(1, xb)
        spread(0, xa, aa)

        @pl.loop(0, chunks // 2 - 1)
        def _(i):
            n = 2 * i
            spread(n + 1, xb, ab)
            gather_outer(n + 2, xa)
            scatter(n, aa)
            spread(n + 2, xa, aa)
            gather_outer(n + 3, xb)
            scatter(n + 1, ab)

        spread(chunks - 1, xb, ab)
        scatter(chunks - 2, aa)
        scatter(chunks - 1, ab)
        part[step] = acc[0:half, :] + acc[half:, :]

        @pl.when(step < last)
        def _():
            begin(step)
            advance(step, slice(pair, half - pair), part[step, pair : half - pair, :])

    for d in range(1, cols):
        gather_copy(d).wait()

    gram = jnp.zeros((cols * width, 2 * width), F32)
    for g in range(groups):
        rows = slice(g * width, (g + 1) * width)
        mine = part[last, rows, :]
        if 0 < g < groups - 1:
            mine = jnp.concatenate([vcur[rows, :], mine], axis=0)
        else:
            mine = jnp.concatenate([jnp.zeros_like(mine), mine], axis=0)
        all_rows = jnp.concatenate([vcur[rows, :]] + [gath[d, rows, :] for d in range(cols - 1)], axis=0)
        mine_high, mine_low = split(mine)
        all_high, all_low = split(all_rows)
        gram += dot_nt(all_high, mine_high) + dot_nt(all_high, mine_low) + dot_nt(all_low, mine_high)
    gram = gram * (1.0 / (parts * owned))
    gsum[...] = jnp.zeros_like(gsum)
    for d in range(cols):
        group = lax.rem(q + cols - d, cols)
        gsum[pl.ds(pl.multiple_of(group * width, width), width), 0 : 2 * width] = gram[d * width : (d + 1) * width]

    def far_copy(d):
        block = lax.rem(z + d, far) * near
        return pltpu.make_async_remote_copy(
            src_ref=gsum.at[pl.ds(pl.multiple_of(block, near), near)],
            dst_ref=got1.at[d],
            send_sem=s1sem.at[d],
            recv_sem=r1sem.at[d],
            device_id=(far_peers[d - 1], q),
            device_id_type=MESH,
        )

    def near_copy(d):
        return pltpu.make_async_remote_copy(
            src_ref=mid,
            dst_ref=got2.at[d],
            send_sem=s2sem.at[d],
            recv_sem=r2sem.at[d],
            device_id=(near_peers[d - 1], q),
            device_id_type=MESH,
        )

    for d in range(1, far):
        far_copy(d).start()

    for t in range(owned // LANES):
        index = jnp.broadcast_to(tab[t : t + 1, :], (width, LANES))
        low = index & (LANES - 1)
        tile = index >> 7
        value = None
        for s in range(2, tiles - 2):
            source = vcur[(s // 2) * width : (s // 2 + 1) * width, (s % 2) * LANES : (s % 2 + 1) * LANES]
            got = pick(source, low)
            value = got if value is None else jnp.where(tile == s, got, value)
        out_filtered[:, t * LANES : (t + 1) * LANES] = value

    value = gsum[pl.ds(pl.multiple_of(z * near, near), near), :]
    for d in range(1, far):
        far_copy(d).wait()
        value += got1[d]
    mid[...] = value
    for d in range(1, near):
        near_copy(d).start()
    for d in range(1, near):
        near_copy(d).wait()
        value += got2[d]
    got2[0] = value
    row = got2[0, pl.ds(yc, 1), :]
    out_corr[...] = row[:, 0:width]
    out_proj[...] = row[:, width : 2 * width]


def per_device(
    start_block, stiffness, cell_scale, node_weight, cell_count, conn, send_rows, filter_bounds
):
    width, owned = start_block.shape
    ghost = send_rows.shape[1]
    npc, cells = conn.shape
    parts = lax.axis_size("cells")
    cols = lax.axis_size("cols")
    inner = parts // 8
    far = parts // inner
    slots = -(-npc // LANES) * LANES
    half = (owned + 2 * ghost) // ghost * width
    steps = DEGREE + 2
    cfg = (width, owned, ghost, npc, cells, parts, cols, inner)
    vmem = pl.BlockSpec(memory_space=pltpu.VMEM)
    smem = pl.BlockSpec(memory_space=pltpu.SMEM)
    dma = pltpu.SemaphoreType.DMA
    rows = cols * width // parts
    return pl.pallas_call(
        functools.partial(kernel, cfg),
        out_shape=(
            jax.ShapeDtypeStruct((width, owned), F32),
            jax.ShapeDtypeStruct((rows, width), F32),
            jax.ShapeDtypeStruct((rows, width), F32),
        ),
        in_specs=[vmem, vmem, vmem, vmem, smem, vmem, vmem, smem],
        out_specs=(vmem, vmem, vmem),
        scratch_shapes=[
            pltpu.VMEM((slots, slots), F32),
            pltpu.VMEM((3 * slots, slots), BF16),
            pltpu.VMEM((cells, slots), I32),
            pltpu.VMEM((16, LANES), I32),
            pltpu.VMEM((LANES, LANES), F32),
            pltpu.VMEM((cells, slots), F32),
            pltpu.VMEM((cells, slots), F32),
            pltpu.VMEM((ghost, cells * slots), BF16),
            pltpu.VMEM((cells * half, slots), BF16),
            pltpu.VMEM((half, ghost), F32),
            pltpu.VMEM((half, ghost), F32),
            pltpu.VMEM((cells * width, slots), F32),
            pltpu.VMEM((CHUNK * width, slots), F32),
            pltpu.VMEM((CHUNK * width, slots), F32),
            pltpu.VMEM((2 * half, CHUNK * slots), BF16),
            pltpu.VMEM((2 * half, CHUNK * slots), BF16),
            pltpu.VMEM((2 * half, ghost), F32),
            pltpu.VMEM((steps, half, ghost), F32),
            pltpu.VMEM((steps, 2 * width, ghost), F32),
            pltpu.VMEM((steps, 2 * width, ghost), F32),
            pltpu.VMEM((cols - 1, half, ghost), F32),
            pltpu.VMEM((width * cols, LANES), F32),
            pltpu.VMEM((far, inner, LANES), F32),
            pltpu.VMEM((inner, LANES), F32),
            pltpu.VMEM((inner, inner, LANES), F32),
            dma((2, steps)),
            dma((2, steps)),
            dma((cols,)),
            dma((cols,)),
            dma((far,)),
            dma((far,)),
            dma((inner,)),
            dma((inner,)),
        ],
        compiler_params=pltpu.CompilerParams(
            collective_id=0, has_side_effects=True, vmem_limit_bytes=52 * 1024 * 1024
        ),
    )(
        start_block,
        stiffness,
        cell_scale.reshape(1, cells),
        node_weight.T,
        cell_count.reshape(1, 1),
        conn.T,
        send_rows,
        filter_bounds.reshape(1, 2),
    )


def solution(mesh):
    placed = (
        P("cols", "cells"),
        P(),
        P("cells"),
        P(None, "cells"),
        P("cells"),
        P(None, "cells"),
        P("cells", None),
        P(),
    )
    return jax.shard_map(
        per_device,
        mesh=mesh,
        in_specs=placed,
        out_specs=(P("cols", "cells"), P("cells", "cols"), P("cells", "cols")),
        check_vma=False,
    )
```

time: 113 us -> 93.8 us (0.83)
  Pallas kernels: 107 us -> 86.2 us
  local copies, waits for them, and re-layouts: 4.61 us -> 6.05 us
    pallas_call x1, Pallas kernels: 107 us -> 86.2 us  [per_device(): pl.pallas_call(functools.partial(kernel, cfg), out_shape=(jax.ShapeDtypeS...]
    unnamed x15 -> x17, local copies, waits for them, and re-layouts: 4.61 us -> 6.05 us
where the time goes in v2:
time: 93.8 us; the launch traced here: 93.5 us
  Pallas kernels  86.2 us (92%)
  local copies, waits for them, and re-layouts  6.05 us (6%)
  between operations  1.32 us (1%)
    pallas_call x1, Pallas kernels, per_device(): pl.pallas_call(functools.partial(kernel, cfg), out_shape=(jax.ShapeDtypeS...  86.2 us
    unnamed x17, local copies, waits for them, and re-layouts  6.05 us

profile of v2, /device:TPU:1, one launch (start us, length us, event | category | flops | bytes accessed | tf_op | source)
XLA Modules:
  0.0 93.5 jit_solution(10550939795253109226)
XLA Ops:
  1.3 0.0 copy-start.4
  1.3 0.0 copy-start.5
  1.3 0.0 copy-start.6
  1.3 0.7 copy-done.4
  2.0 0.0 copy-done.5
  2.0 0.0 copy-done.6
  2.0 0.0 copy-start
  2.0 1.0 %copy-done = f32[343,343]{1,0:T(8,128)S(1)} copy-done((f32[343,343]{1,0:T(8,128)S(1)}, f32[343,343]{1,0:T(8,128)}, u32[]{:S(2)}) %copy-start) | copy-done | bytes 470620
  3.0 0.0 copy-start.1
  3.0 0.9 copy-done.1
  3.9 0.0 copy-start.2
  3.9 0.9 copy-done.2
  4.8 0.0 copy-start.3
  4.8 0.9 copy-done.3
  5.7 86.2 %shard_map.103 = (f32[16,1536]{1,0:T(8,128)S(1)}, f32[1,16]{1,0:T(1,128)S(1)}, f32[1,16]{1,0:T(1,128)S(1)}) custom-call(f32[16,1536]{1,0:T(8,128)S(1)} %copy-done.1, f32[343,343]{1,0:T(8,128)S(1)} %copy-done, f32[1,64]{1,0:T(1,128)S(1)} %bitcast.8, f32[64,343]{1,0:T(8,128)S(1)} %bitcast.6, s32[1,1]{1,0:T(1,128)} %bitcast.5.count, s32[64,343]{1,0:T(8,128)S(1)} %bitcast.7, ...), custom_call_target="tpu_custom_call" | custom-call | tf_op jit(solution)/shard_map/pallas_call | solution.py:446
  91.9 0.6 copy.15
  92.5 0.5 copy.16
  93.0 0.5 copy.17
Async XLA Ops:
  1.3 0.7 copy-start.4
  1.3 0.7 copy-start.5
  1.3 0.7 copy-start.6
  2.0 1.0 %copy-start = (f32[343,343]{1,0:T(8,128)S(1)}, f32[343,343]{1,0:T(8,128)}, u32[]{:S(2)}) copy-start(f32[343,343]{1,0:T(8,128)} %stiff.1) | copy-start | bytes 1411792
  3.0 0.9 copy-start.1
  3.9 0.9 copy-start.2
  4.8 0.9 copy-start.3

commit v3 on v2

--- a/solution.py
+++ b/solution.py
@@ -44,17 +44,24 @@
 
 def kernel(
     cfg,
+    start_hbm,
+    stiff_hbm,
+    scale_hbm,
+    weight_hbm,
+    count,
+    conn_hbm,
+    send_hbm,
+    bounds,
+    out_filtered,
+    out_corr,
+    out_proj,
     start,
     stiff,
     scale,
     weight,
-    count,
     conn,
     send,
-    bounds,
-    out_filtered,
-    out_corr,
-    out_proj,
+    insem,
     kpad,
     kk,
     newr,
@@ -77,25 +84,19 @@
     from_right,
     gath,
     gsum,
-    got1,
-    mid,
-    got2,
+    rowbuf,
     ssem,
     rsem,
     gssem,
     grsem,
     s1sem,
     r1sem,
-    s2sem,
-    r2sem,
 ):
-    width, owned, ghost, npc, cells, parts, cols, inner = cfg
+    width, owned, ghost, npc, cells, parts, cols = cfg
     slots = newr.shape[1]
     groups = (owned + 2 * ghost) // ghost
     half = groups * width
     tiles = 2 * groups
-    near = inner
-    far = parts // inner
     pair = 2 * width
     chunks = cells // CHUNK
     span = CHUNK * slots
@@ -104,21 +105,33 @@
     q = lax.axis_index("cols")
     left = lax.rem(p + parts - 1, parts)
     right = lax.rem(p + 1, parts)
-    z = lax.div(p, near)
-    yc = lax.rem(p, near)
-
-    far_peers = [lax.rem(z + d, far) * near + yc for d in range(1, far)]
-    near_peers = [z * near + lax.rem(yc + d, near) for d in range(1, near)]
     col_peers = [lax.rem(q + d, cols) for d in range(1, cols)]
 
+    loads = [
+        pltpu.make_async_copy(source, target, insem.at[i])
+        for i, (source, target) in enumerate(
+            [
+                (send_hbm, send),
+                (conn_hbm, conn),
+                (start_hbm, start),
+                (scale_hbm, scale),
+                (weight_hbm, weight),
+                (stiff_hbm, stiff),
+            ]
+        )
+    ]
+    for load in loads:
+        load.start()
+
     barrier = pltpu.get_barrier_semaphore()
-    targets = [(left, q), (right, q)]
-    targets += [(p, other) for other in col_peers]
-    targets += [(other, q) for other in far_peers]
-    targets += [(other, q) for other in near_peers]
-    for target in targets:
-        pl.semaphore_signal(barrier, inc=1, device_id=target, device_id_type=MESH)
-
+    for other in col_peers:
+        pl.semaphore_signal(barrier, inc=1, device_id=(p, other), device_id_type=MESH)
+
+    @pl.loop(1, parts)
+    def _(d):
+        pl.semaphore_signal(barrier, inc=1, device_id=(lax.rem(p + d, parts), q), device_id_type=MESH)
+
+    loads[0].wait()
     lane = iota((1, LANES), 1)
     per_side = owned // 2 // LANES
     rows_nm[...] = jnp.zeros_like(rows_nm)
@@ -151,6 +164,7 @@
 
     tab_cols = jnp.concatenate([tab[...], jnp.zeros((LANES - tiles, LANES), I32)], axis=0).astype(F32).T.astype(I32)
     total = jnp.zeros((2 * half, ghost), F32)
+    loads[2].wait()
     for t in range(owned // LANES):
         high, low = split(start[:, t * LANES : (t + 1) * LANES])
         group = jnp.broadcast_to(tab[t : t + 1, :] >> 8, (half, LANES))
@@ -210,12 +224,11 @@
         d = (part[step, half - width : half, :] + from_right[step, width:pair, :]) * has_right
         advance(step, slice(half - pair, half), jnp.concatenate([c, d], axis=0))
 
-    pl.semaphore_wait(barrier, len(targets))
-    begin(0)
     vcur[...] = jnp.zeros_like(vcur)
     vprev[...] = jnp.zeros_like(vprev)
     advance(0, slice(pair, half - pair), part[0, pair : half - pair, :])
 
+    loads[5].wait()
     kpad[...] = jnp.zeros_like(kpad)
     kpad[0:npc, 0:npc] = stiff[...]
     k_high, k_low = split(kpad[...].T)
@@ -223,6 +236,7 @@
     kk[slots : 2 * slots, :] = k_high
     kk[2 * slots :, :] = k_low
 
+    loads[1].wait()
     newr[...] = jnp.zeros_like(newr)
     newr[:, 0:npc] = conn[...]
     for l in range(slots // LANES):
@@ -236,6 +250,8 @@
         newr[:, l * LANES : (l + 1) * LANES] = value
 
     live = mark(iota((cells, slots), 0) < count[0, 0]) * (1.0 / MULT)
+    loads[3].wait()
+    loads[4].wait()
     wt[...] = jnp.zeros_like(wt)
     wt[:, 0:npc] = weight[...]
     wt[...] = wt[...] * live
@@ -256,6 +272,9 @@
         masks[pl.ds(pl.multiple_of(c * half, half), half), :] = jnp.where(
             member, jnp.ones((), BF16), jnp.zeros((), BF16)
         )
+
+    pl.semaphore_wait(barrier, parts + cols - 2)
+    begin(0)
 
     inner_tiles = range(4, tiles - 4)
     outer_tiles = list(range(4)) + list(range(tiles - 4, tiles))
@@ -374,29 +393,21 @@
         group = lax.rem(q + cols - d, cols)
         gsum[pl.ds(pl.multiple_of(group * width, width), width), 0 : 2 * width] = gram[d * width : (d + 1) * width]
 
-    def far_copy(d):
-        block = lax.rem(z + d, far) * near
+    def row_copy(d):
         return pltpu.make_async_remote_copy(
-            src_ref=gsum.at[pl.ds(pl.multiple_of(block, near), near)],
-            dst_ref=got1.at[d],
+            src_ref=gsum.at[pl.ds(lax.rem(p + d, parts), 1)],
+            dst_ref=rowbuf.at[d],
             send_sem=s1sem.at[d],
             recv_sem=r1sem.at[d],
-            device_id=(far_peers[d - 1], q),
+            device_id=(lax.rem(p + d, parts), q),
             device_id_type=MESH,
         )
 
-    def near_copy(d):
-        return pltpu.make_async_remote_copy(
-            src_ref=mid,
-            dst_ref=got2.at[d],
-            send_sem=s2sem.at[d],
-            recv_sem=r2sem.at[d],
-            device_id=(near_peers[d - 1], q),
-            device_id_type=MESH,
-        )
-
-    for d in range(1, far):
-        far_copy(d).start()
+    @pl.loop(1, parts)
+    def _(d):
+        row_copy(d).start()
+
+    rowbuf[0] = gsum[pl.ds(p, 1), :]
 
     for t in range(owned // LANES):
         index = jnp.broadcast_to(tab[t : t + 1, :], (width, LANES))
@@ -409,18 +420,11 @@
             value = got if value is None else jnp.where(tile == s, got, value)
         out_filtered[:, t * LANES : (t + 1) * LANES] = value
 
-    value = gsum[pl.ds(pl.multiple_of(z * near, near), near), :]
-    for d in range(1, far):
-        far_copy(d).wait()
-        value += got1[d]
-    mid[...] = value
-    for d in range(1, near):
-        near_copy(d).start()
-    for d in range(1, near):
-        near_copy(d).wait()
-        value += got2[d]
-    got2[0] = value
-    row = got2[0, pl.ds(yc, 1), :]
+    @pl.loop(1, parts)
+    def _(d):
+        row_copy(d).wait()
+
+    row = jnp.sum(rowbuf[...], axis=0)
     out_corr[...] = row[:, 0:width]
     out_proj[...] = row[:, width : 2 * width]
 
@@ -433,13 +437,12 @@
     npc, cells = conn.shape
     parts = lax.axis_size("cells")
     cols = lax.axis_size("cols")
-    inner = parts // 8
-    far = parts // inner
     slots = -(-npc // LANES) * LANES
     half = (owned + 2 * ghost) // ghost * width
     steps = DEGREE + 2
-    cfg = (width, owned, ghost, npc, cells, parts, cols, inner)
+    cfg = (width, owned, ghost, npc, cells, parts, cols)
     vmem = pl.BlockSpec(memory_space=pltpu.VMEM)
+    hbm = pl.BlockSpec(memory_space=pltpu.HBM)
     smem = pl.BlockSpec(memory_space=pltpu.SMEM)
     dma = pltpu.SemaphoreType.DMA
     rows = cols * width // parts
@@ -450,9 +453,16 @@
             jax.ShapeDtypeStruct((rows, width), F32),
             jax.ShapeDtypeStruct((rows, width), F32),
         ),
-        in_specs=[vmem, vmem, vmem, vmem, smem, vmem, vmem, smem],
+        in_specs=[hbm, hbm, hbm, hbm, smem, hbm, hbm, smem],
         out_specs=(vmem, vmem, vmem),
         scratch_shapes=[
+            pltpu.VMEM((width, owned), F32),
+            pltpu.VMEM((npc, npc), F32),
+            pltpu.VMEM((1, cells), F32),
+            pltpu.VMEM((cells, npc), F32),
+            pltpu.VMEM((cells, npc), I32),
+            pltpu.VMEM((2, ghost), I32),
+            dma((6,)),
             pltpu.VMEM((slots, slots), F32),
             pltpu.VMEM((3 * slots, slots), BF16),
             pltpu.VMEM((cells, slots), I32),
@@ -475,20 +485,16 @@
             pltpu.VMEM((steps, 2 * width, ghost), F32),
             pltpu.VMEM((cols - 1, half, ghost), F32),
             pltpu.VMEM((width * cols, LANES), F32),
-            pltpu.VMEM((far, inner, LANES), F32),
-            pltpu.VMEM((inner, LANES), F32),
-            pltpu.VMEM((inner, inner, LANES), F32),
+            pltpu.VMEM((parts, 1, LANES), F32),
             dma((2, steps)),
             dma((2, steps)),
             dma((cols,)),
             dma((cols,)),
-            dma((far,)),
-            dma((far,)),
-            dma((inner,)),
-            dma((inner,)),
+            dma((parts,)),
+            dma((parts,)),
         ],
         compiler_params=pltpu.CompilerParams(
-            collective_id=0, has_side_effects=True, vmem_limit_bytes=52 * 1024 * 1024
+            collective_id=0, has_side_effects=True, vmem_limit_bytes=62 * 1024 * 1024
         ),
     )(
         start_block,

time: 93.8 us -> 89.8 us (0.957)
  local copies, waits for them, and re-layouts: 6.05 us -> 2.71 us
    unnamed x17 -> x7, local copies, waits for them, and re-layouts: 6.05 us -> 2.71 us
where the time goes in v3:
time: 89.8 us; the launch traced here: 89.7 us
  Pallas kernels  85.7 us (95%)
  local copies, waits for them, and re-layouts  2.71 us (3%)
  between operations  1.3 us (1%)
    pallas_call x1, Pallas kernels, per_device(): pl.pallas_call(functools.partial(kernel, cfg), out_shape=(jax.ShapeDtypeS...  85.7 us
    unnamed x7, local copies, waits for them, and re-layouts  2.71 us

profile of v3, /device:TPU:1, one launch (start us, length us, event | category | flops | bytes accessed | tf_op | source)
XLA Modules:
  0.0 89.7 jit_solution(93250441860748836)
XLA Ops:
  1.3 85.7 %shard_map.103 = (f32[16,1536]{1,0:T(8,128)}, f32[1,16]{1,0:T(1,128)}, f32[1,16]{1,0:T(1,128)}) custom-call(f32[16,1536]{1,0:T(8,128)} %start_hbm.1, f32[343,343]{1,0:T(8,128)} %stiff_hbm.1, f32[1,64]{1,0:T(1,128)} %bitcast.8, f32[64,343]{1,0:T(8,128)} %bitcast.6, s32[1,1]{1,0:T(1,128)} %bitcast.5.count, s32[64,343]{1,0:T(8,128)} %bitcast.7, ...), custom_call_target="tpu_custom_call" | custom-call | tf_op jit(solution)/shard_map/pallas_call | solution.py:449
  87.0 0.0 copy-start.1
  87.0 1.5 %copy.15 = f32[16,1536]{1,0:T(8,128)} copy(f32[16,1536]{1,0:T(8,128)} %get-tuple-element.6) | data formatting | bytes 196608
  88.5 0.0 copy-done.1
  88.5 0.0 copy-start
  88.5 0.5 copy.16
  89.1 0.1 copy-done
  89.2 0.5 copy.17
Async XLA Ops:
  87.0 1.6 %copy-start.1 = (f32[1,16]{1,0:T(1,128)S(1)}, f32[1,16]{1,0:T(1,128)}, u32[]{:S(2)}) copy-start(f32[1,16]{1,0:T(1,128)} %get-tuple-element.7) | copy-start | bytes 196
  88.5 0.7 copy-start

commit v4 on v3

--- a/solution.py
+++ b/solution.py
@@ -65,6 +65,9 @@
     kpad,
     kk,
     newr,
+    index8,
+    weight8,
+    scale8,
     tab,
     rows_nm,
     wt,
@@ -262,6 +265,10 @@
     @pl.loop(0, cells)
     def _(c):
         index = newr[pl.ds(c, 1), :]
+        rows = pl.ds(pl.multiple_of(c * 8, 8), 8)
+        index8[rows, :] = jnp.broadcast_to(index, (8, slots))
+        weight8[rows, :] = jnp.broadcast_to(wt[pl.ds(c, 1), :], (8, slots))
+        scale8[rows, :] = jnp.broadcast_to(sc[pl.ds(c, 1), :], (8, slots))
         place = (index & (ghost - 1)).astype(F32).astype(BF16)
         hit = jnp.broadcast_to(place, (ghost, slots)) == iota((ghost, slots), 0).astype(F32).astype(BF16)
         onehot[:, pl.ds(pl.multiple_of(c * slots, LANES), slots)] = jnp.where(
@@ -279,8 +286,11 @@
     inner_tiles = range(4, tiles - 4)
     outer_tiles = list(range(4)) + list(range(tiles - 4, tiles))
 
+    def twice(x):
+        return jnp.concatenate([x, x], axis=0)
+
     def collect(cell, group, which, value):
-        index = jnp.broadcast_to(newr[pl.ds(cell, 1), :][:, group * LANES : (group + 1) * LANES], (width, LANES))
+        index = twice(index8[pl.ds(pl.multiple_of(cell * 8, 8), 8), group * LANES : (group + 1) * LANES])
         low = index & (LANES - 1)
         tile = index >> 7
         for t in which:
@@ -291,9 +301,13 @@
     def rows_of(cell):
         return pl.ds(pl.multiple_of(cell * width, width), width)
 
-    def gather_inner(chunk):
-        for c in range(CHUNK):
-            cell = chunk * CHUNK + c
+    turns = chunks // 2 - 1
+    late = 3 * turns
+    early = cells - late
+
+    def gather_inner(first, number):
+        for c in range(number):
+            cell = first + c
             for l in range(slots // LANES):
                 value = collect(cell, l, inner_tiles, jnp.zeros((width, LANES), F32))
                 xall[rows_of(cell), l * LANES : (l + 1) * LANES] = value
@@ -312,7 +326,8 @@
         for c in range(CHUNK):
             cell = chunk * CHUNK + c
             rows = slice(c * width, (c + 1) * width)
-            term = wide[rows] * sc[pl.ds(cell, 1), :] + local[rows] * wt[pl.ds(cell, 1), :]
+            eight = pl.ds(pl.multiple_of(cell * 8, 8), 8)
+            term = wide[rows] * twice(scale8[eight, :]) + local[rows] * twice(weight8[eight, :])
             high, low = split(term)
             for g in range(groups):
                 member = masks[pl.ds(pl.multiple_of(cell * half + g * width, width), width), :]
@@ -336,9 +351,9 @@
 
     @pl.loop(1, last + 1)
     def _(step):
-        @pl.loop(0, chunks)
+        @pl.loop(0, early // 5)
         def _(i):
-            gather_inner(i)
+            gather_inner(i * 5, 5)
 
         finish(step - 1)
 
@@ -355,6 +370,7 @@
         @pl.loop(0, chunks // 2 - 1)
         def _(i):
             n = 2 * i
+            gather_inner(early + 3 * i, 3)
             spread(n + 1, xb, ab)
             gather_outer(n + 2, xa)
             scatter(n, aa)
@@ -397,15 +413,19 @@
         return pltpu.make_async_remote_copy(
             src_ref=gsum.at[pl.ds(lax.rem(p + d, parts), 1)],
             dst_ref=rowbuf.at[d],
-            send_sem=s1sem.at[d],
-            recv_sem=r1sem.at[d],
+            send_sem=s1sem,
+            recv_sem=r1sem,
             device_id=(lax.rem(p + d, parts), q),
             device_id_type=MESH,
         )
 
-    @pl.loop(1, parts)
-    def _(d):
-        row_copy(d).start()
+    middle = parts // 2
+    row_copy(middle).start()
+
+    @pl.loop(1, middle)
+    def _(j):
+        row_copy(middle - j).start()
+        row_copy(middle + j).start()
 
     rowbuf[0] = gsum[pl.ds(p, 1), :]
 
@@ -420,10 +440,16 @@
             value = got if value is None else jnp.where(tile == s, got, value)
         out_filtered[:, t * LANES : (t + 1) * LANES] = value
 
-    @pl.loop(1, parts)
-    def _(d):
-        row_copy(d).wait()
-
+    every = pltpu.make_async_remote_copy(
+        src_ref=rowbuf.at[pl.ds(1, parts - 1)],
+        dst_ref=rowbuf.at[pl.ds(1, parts - 1)],
+        send_sem=s1sem,
+        recv_sem=r1sem,
+        device_id=(right, q),
+        device_id_type=MESH,
+    )
+    every.wait_send()
+    every.wait_recv()
     row = jnp.sum(rowbuf[...], axis=0)
     out_corr[...] = row[:, 0:width]
     out_proj[...] = row[:, width : 2 * width]
@@ -466,6 +492,9 @@
             pltpu.VMEM((slots, slots), F32),
             pltpu.VMEM((3 * slots, slots), BF16),
             pltpu.VMEM((cells, slots), I32),
+            pltpu.VMEM((cells * 8, slots), I32),
+            pltpu.VMEM((cells * 8, slots), F32),
+            pltpu.VMEM((cells * 8, slots), F32),
             pltpu.VMEM((16, LANES), I32),
             pltpu.VMEM((LANES, LANES), F32),
             pltpu.VMEM((cells, slots), F32),
@@ -490,8 +519,8 @@
             dma((2, steps)),
             dma((cols,)),
             dma((cols,)),
-            dma((parts,)),
-            dma((parts,)),
+            dma,
+            dma,
         ],
         compiler_params=pltpu.CompilerParams(
             collective_id=0, has_side_effects=True, vmem_limit_bytes=62 * 1024 * 1024

time: 89.8 us -> 86.7 us (0.965)
  Pallas kernels: 85.7 us -> 82.6 us
    pallas_call x1, Pallas kernels: 85.7 us -> 82.6 us  [per_device(): pl.pallas_call(functools.partial(kernel, cfg), out_shape=(jax.ShapeDtypeS...]
where the time goes in v4:
time: 86.7 us; the launch traced here: 86.6 us
  Pallas kernels  82.6 us (95%)
  local copies, waits for them, and re-layouts  2.71 us (3%)
  between operations  1.3 us (1%)
    pallas_call x1, Pallas kernels, per_device(): pl.pallas_call(functools.partial(kernel, cfg), out_shape=(jax.ShapeDtypeS...  82.6 us
    unnamed x7, local copies, waits for them, and re-layouts  2.71 us

profile of v4, /device:TPU:1, one launch (start us, length us, event | category | flops | bytes accessed | tf_op | source)
XLA Modules:
  0.0 86.6 jit_solution(7753700419609398662)
XLA Ops:
  1.3 82.6 %shard_map.103 = (f32[16,1536]{1,0:T(8,128)}, f32[1,16]{1,0:T(1,128)}, f32[1,16]{1,0:T(1,128)}) custom-call(f32[16,1536]{1,0:T(8,128)} %start_hbm.1, f32[343,343]{1,0:T(8,128)} %stiff_hbm.1, f32[1,64]{1,0:T(1,128)} %bitcast.8, f32[64,343]{1,0:T(8,128)} %bitcast.6, s32[1,1]{1,0:T(1,128)} %bitcast.5.count, s32[64,343]{1,0:T(8,128)} %bitcast.7, ...), custom_call_target="tpu_custom_call" | custom-call | tf_op jit(solution)/shard_map/pallas_call | solution.py:475
  83.9 0.0 copy-start.1
  83.9 1.5 %copy.15 = f32[16,1536]{1,0:T(8,128)} copy(f32[16,1536]{1,0:T(8,128)} %get-tuple-element.6) | data formatting | bytes 196608
  85.4 0.0 copy-done.1
  85.4 0.0 copy-start
  85.4 0.5 copy.16
  85.9 0.1 copy-done
  86.1 0.5 copy.17
Async XLA Ops:
  83.9 1.6 %copy-start.1 = (f32[1,16]{1,0:T(1,128)S(1)}, f32[1,16]{1,0:T(1,128)}, u32[]{:S(2)}) copy-start(f32[1,16]{1,0:T(1,128)} %get-tuple-element.7) | copy-start | bytes 196
  85.4 0.7 copy-start

commit v5 on v4

--- a/solution.py
+++ b/solution.py
@@ -55,6 +55,8 @@
     out_filtered,
     out_corr,
     out_proj,
+    ordered,
+    outsem,
     start,
     stiff,
     scale,
@@ -130,8 +132,7 @@
     for other in col_peers:
         pl.semaphore_signal(barrier, inc=1, device_id=(p, other), device_id_type=MESH)
 
-    @pl.loop(1, parts)
-    def _(d):
+    for d in range(1, parts):
         pl.semaphore_signal(barrier, inc=1, device_id=(lax.rem(p + d, parts), q), device_id_type=MESH)
 
     loads[0].wait()
@@ -302,7 +303,7 @@
         return pl.ds(pl.multiple_of(cell * width, width), width)
 
     turns = chunks // 2 - 1
-    late = 3 * turns
+    late = 6 * turns
     early = cells - late
 
     def gather_inner(first, number):
@@ -351,9 +352,9 @@
 
     @pl.loop(1, last + 1)
     def _(step):
-        @pl.loop(0, early // 5)
+        @pl.loop(0, early // 23)
         def _(i):
-            gather_inner(i * 5, 5)
+            gather_inner(i * 23, 23)
 
         finish(step - 1)
 
@@ -370,7 +371,7 @@
         @pl.loop(0, chunks // 2 - 1)
         def _(i):
             n = 2 * i
-            gather_inner(early + 3 * i, 3)
+            gather_inner(early + 6 * i, 6)
             spread(n + 1, xb, ab)
             gather_outer(n + 2, xa)
             scatter(n, aa)
@@ -438,7 +439,9 @@
             source = vcur[(s // 2) * width : (s // 2 + 1) * width, (s % 2) * LANES : (s % 2 + 1) * LANES]
             got = pick(source, low)
             value = got if value is None else jnp.where(tile == s, got, value)
-        out_filtered[:, t * LANES : (t + 1) * LANES] = value
+        ordered[:, t * LANES : (t + 1) * LANES] = value
+    store = pltpu.make_async_copy(ordered, out_filtered, outsem)
+    store.start()
 
     every = pltpu.make_async_remote_copy(
         src_ref=rowbuf.at[pl.ds(1, parts - 1)],
@@ -448,6 +451,7 @@
         device_id=(right, q),
         device_id_type=MESH,
     )
+    store.wait()
     every.wait_send()
     every.wait_recv()
     row = jnp.sum(rowbuf[...], axis=0)
@@ -480,8 +484,10 @@
             jax.ShapeDtypeStruct((rows, width), F32),
         ),
         in_specs=[hbm, hbm, hbm, hbm, smem, hbm, hbm, smem],
-        out_specs=(vmem, vmem, vmem),
+        out_specs=(hbm, vmem, vmem),
         scratch_shapes=[
+            pltpu.VMEM((width, owned), F32),
+            dma,
             pltpu.VMEM((width, owned), F32),
             pltpu.VMEM((npc, npc), F32),
             pltpu.VMEM((1, cells), F32),

time: 86.7 us -> 82.8 us (0.955)
  Pallas kernels: 82.6 us -> 78.7 us
    pallas_call x1, Pallas kernels: 82.6 us -> 78.7 us  [per_device(): pl.pallas_call(functools.partial(kernel, cfg), out_shape=(jax.ShapeDtypeS...]
where the time goes in v5:
time: 82.8 us; the launch traced here: 82.7 us
  Pallas kernels  78.7 us (95%)
  local copies, waits for them, and re-layouts  2.71 us (3%)
  between operations  1.3 us (2%)
    pallas_call x1, Pallas kernels, per_device(): pl.pallas_call(functools.partial(kernel, cfg), out_shape=(jax.ShapeDtypeS...  78.7 us
    unnamed x7, local copies, waits for them, and re-layouts  2.71 us

profile of v5, /device:TPU:1, one launch (start us, length us, event | category | flops | bytes accessed | tf_op | source)
XLA Modules:
  0.0 82.7 jit_solution(3035543274716374372)
XLA Ops:
  1.3 78.7 %shard_map.103 = (f32[16,1536]{1,0:T(8,128)}, f32[1,16]{1,0:T(1,128)}, f32[1,16]{1,0:T(1,128)}) custom-call(f32[16,1536]{1,0:T(8,128)} %start_hbm.1, f32[343,343]{1,0:T(8,128)} %stiff_hbm.1, f32[1,64]{1,0:T(1,128)} %bitcast.8, f32[64,343]{1,0:T(8,128)} %bitcast.6, s32[1,1]{1,0:T(1,128)} %bitcast.5.count, s32[64,343]{1,0:T(8,128)} %bitcast.7, ...), custom_call_target="tpu_custom_call" | custom-call | tf_op jit(solution)/shard_map/pallas_call | solution.py:479
  80.0 0.0 copy-start.1
  80.0 1.5 %copy.15 = f32[16,1536]{1,0:T(8,128)} copy(f32[16,1536]{1,0:T(8,128)} %get-tuple-element.6) | data formatting | bytes 196608
  81.5 0.0 copy-done.1
  81.5 0.0 copy-start
  81.5 0.5 copy.16
  82.0 0.1 copy-done
  82.2 0.5 copy.17
Async XLA Ops:
  80.0 1.6 %copy-start.1 = (f32[1,16]{1,0:T(1,128)S(1)}, f32[1,16]{1,0:T(1,128)}, u32[]{:S(2)}) copy-start(f32[1,16]{1,0:T(1,128)} %get-tuple-element.7) | copy-start | bytes 196
  81.5 0.7 copy-start
